TPU v7x, 256 devices: a whole 4x4x8 slice. The times are simulated.
256 devices in a mesh: rad: 16 (over x, y_hi, core), fn: 16 (over y_lo, z).
Axes of the slice: x: 4, y: 4 (y_hi: 2, y_lo: 2; y = y_hi * 2 + y_lo), z: 8, core: 2. Of those that a mesh axis runs over, the one named last changes fastest.
Arguments:
- functions: bfloat16 [256, 640, 1202], P('fn', 'rad'), may hold values from -6 to 6
- orbital: float32 [640, 1202], P('rad'), may hold values from -6 to 6
- radial_weight: float32 [640], P('rad'), may hold values from 0.5 to 2
- ylm: bfloat16 [961, 1202], replicated, may hold values from -0.15625 to 0.15625
Outputs:
- potential: bfloat16 [256, 640, 1202], P('fn', 'rad')
- exchange_kernel: float32 [256, 256], P('rad', 'fn')
All inputs are finite; a program needn't handle non-finite values.
Results may differ from a plain program's by a relative error of at most 0.0065.
Values may be sent and summed in bfloat16 or wider, within the bound.
A program may use at most 128 MiB of HBM per device.

v0:
```python
import math

import jax
import jax.numpy as jnp
import numpy as np
from jax import lax
from jax.sharding import PartitionSpec as P

LMAX = 30


def degrees():
    table = np.repeat(np.arange(LMAX + 1), 2 * np.arange(LMAX + 1) + 1)
    return jnp.asarray(table, jnp.float32)


def local_green(weighted, radius, degree):
    count = radius.shape[0]
    source = weighted.astype(jnp.float32) / radius[None, :, None]
    logr = jnp.log(radius)[:, None]
    grow = jnp.exp((degree[None, :] + 1.0) * logr)
    shrink = jnp.exp(-degree[None, :] * logr)
    rows = jnp.arange(count, dtype=jnp.int32)
    lower = (rows[None, :] <= rows[:, None]).astype(jnp.float32)
    upper = (rows[None, :] >= rows[:, None]).astype(jnp.float32)
    grown = source * grow[None]
    shrunk = source * shrink[None]
    out_sum = jnp.einsum("ij,fjm->fim", lower, grown, precision=lax.Precision.HIGHEST)
    in_sum = jnp.einsum("ij,fjm->fim", upper, shrunk, precision=lax.Precision.HIGHEST)
    return (out_sum, in_sum, source, grow, shrink, grown, shrunk)


def local(functions, orbital, radial_weight, ylm):
    local_funcs, local_radial, angle_count = functions.shape
    radial_devices = lax.axis_size("rad")
    total_radial = local_radial * radial_devices
    spacing = 3.0 / total_radial
    positions = lax.axis_index("rad") * local_radial + jnp.arange(local_radial, dtype=jnp.int32)
    radius = 1.0 + spacing * (positions.astype(jnp.float32) + 0.5)
    quadrature = spacing * radial_weight * radius * radius
    degree = degrees()
    multipole = 4.0 * math.pi / (2.0 * degree + 1.0)
    density = (orbital[None] * functions).astype(jnp.bfloat16)
    projected = lax.dot_general(
        density, ylm, (((2,), (1,)), ((), ())), preferred_element_type=jnp.float32
    )
    weighted = (projected * quadrature[None, :, None]).astype(jnp.bfloat16)
    regrouped = lax.all_to_all(weighted, "rad", split_axis=0, concat_axis=1, tiled=True)
    full_radius = 1.0 + spacing * (jnp.arange(total_radial).astype(jnp.float32) + 0.5)
    out_sum, in_sum, source, grow, shrink, grown, shrunk = local_green(
        regrouped, full_radius, degree
    )
    outward = out_sum / grow[None]
    inward = in_sum / shrink[None]
    grouped = (multipole * (outward + inward - source)).astype(jnp.bfloat16)
    coefficients = lax.all_to_all(grouped, "rad", split_axis=1, concat_axis=0, tiled=True)
    potential = lax.dot_general(
        coefficients, ylm, (((2,), (0,)), ((), ())), preferred_element_type=jnp.float32
    ).astype(jnp.bfloat16)
    flat_coefficients = coefficients.reshape(local_funcs, -1)
    piece = lax.all_gather(weighted, "fn", axis=0, tiled=True)
    rows = lax.dot_general(
        piece.reshape(piece.shape[0], -1),
        flat_coefficients,
        (((1,), (1,)), ((), ())),
        preferred_element_type=jnp.float32,
    )
    partial_kernel = rows
    partial_kernel = partial_kernel * (4.0 * math.pi / angle_count)
    kernel = lax.psum_scatter(partial_kernel, "rad", scatter_dimension=0, tiled=True)
    return (potential, kernel)


def solution(mesh):
    in_specs = (P("fn", "rad", None), P("rad", None), P("rad"), P())
    out_specs = (P("fn", "rad", None), P("rad", "fn"))
    return jax.shard_map(local, mesh=mesh, in_specs=in_specs, out_specs=out_specs, check_vma=False)
```

profile of v0, /device:TPU:1, one launch (start us, length us, event | category | flops | bytes accessed | tf_op | source)
XLA Modules:
  0.0 465.9 jit_solution(1079863812052111060)
XLA Ops:
  7.2 0.0 copy-start
  7.2 0.0 all-gather.2.cloned.1.call-start
  7.2 0.8 multiply_multiply_fusion
  8.0 0.8 copy-done
  8.9 4.4 multiply_convert_fusion.1
  13.3 0.0 all-gather.2.cloned.1.call-update
  13.3 8.5 %all-to-all-start = ((bf16[16,40,961]{2,1,0:T(8,128)(2,1)}), bf16[16,40,961]{2,1,0:T(8,128)(2,1)}, u32[]{:S(2)}, u32[]{:S(2)}) async-start(bf16[16,40,961]{2,1,0:T(8,128)(2,1)} %multiply_convert_fusion.1), calls=%async_computation | async-start | bytes 2621440 | tf_op jit(solution)/shard_map/all_to_all | solution.py:48
  21.7 0.0 reduce-scatter.2.cloned.1.call-start
  21.8 23.3 %all-to-all-done = bf16[16,40,961]{2,1,0:T(8,128)(2,1)} async-done(((bf16[16,40,961]{2,1,0:T(8,128)(2,1)}), bf16[16,40,961]{2,1,0:T(8,128)(2,1)}, u32[]{:S(2)}, u32[]{:S(2)}) %all-to-all-start) | async-done | bytes 1230112 | tf_op jit(solution)/shard_map/all_to_all | solution.py:48
  45.1 3.3 copy.13
  48.4 0.0 copy-start.3
  48.4 1.7 bitcast_divide_fusion
  50.1 0.0 copy-done.3
  50.1 0.0 copy-start.2
  50.1 0.0 copy-start.4
  50.1 0.0 copy-start.5
  50.1 6.5 %fusion = f32[961,640]{1,0:T(8,128)S(1)} fusion(f32[640,961]{1,0:T(8,128)S(1)} %bitcast_divide_fusion, f32[961]{0:T(1024)S(1)} %copy-done.3, f32[640]{0:T(1024)S(1)} %get-tuple-element.3), kind=kOutput, calls=%fused_computation.3 | convolution fusion | flops 4725146624 | bytes 4926724 | tf_op jit(solution)/shard_map/ij,fjm->fim/dot_general | solution.py:29
  56.7 8.6 %fusion.11 = bf16[1,640,961]{1,2,0:T(8,128)(2,1)} fusion(f32[1,640,961]{1,2,0:T(8,128)S(1)} %copy-done.2, f32[961,640]{1,0:T(8,128)S(1)} %fusion, f32[640,961]{1,0:T(8,128)S(1)} %bitcast_divide_fusion, f32[640]{0:T(1024)S(1)} %get-tuple-element.3, f32[961]{0:T(1024)S(1)} %copy-done.4, f32[640]{0:T(1024)S(1)} %get-tuple-element.2, f32[961]{0:T(1024)S(1)} %copy-done.3, ...), kind=kOutput, calls=%fused_computation.17 | convolution fusion | flops 4730682368 | bytes 8627212 | tf_op jit(solution)/shard_map/ij,fjm->fim/dot_general | solution.py:28
  65.3 6.4 %copy.14 = bf16[1,640,961]{2,0,1:T(2,128)(2,1)} copy(bf16[1,640,961]{1,2,0:T(8,128)(2,1)} %fusion.11) | data formatting | bytes 2460160 | tf_op jit(solution)/shard_map/convert_element_type | solution.py:55
  71.6 0.5 broadcast.148
  72.1 11.0 %reduce.2 = bf16[640,961]{1,0:T(8,128)(2,1)} reduce(bf16[640,1,961]{2,1,0:T(2,128)(2,1)} %bitcast.39, bf16[]{:T(256)} %broadcast.148), dimensions={1}, to_apply=%bitcast.32.reduce_sub_computation | reduce | bytes 2460162
  83.1 5.5 %reshape.233 = bf16[16,2,19220]{2,1,0:T(2,128)(2,1)} reshape(bf16[640,961]{1,0:T(8,128)(2,1)} %reduce.2) | data formatting | bytes 2460160
  88.7 229.7 %all_to_all.21 = bf16[16,2,19220]{2,1,0:T(2,128)(2,1)} all-to-all(bf16[16,2,19220]{2,1,0:T(2,128)(2,1)} %reshape.233), channel_id=1, replica_groups=mesh['rad'=16,'fn'=16] {'rad'}, dimensions={0} | all-to-all | bytes 2460160 | tf_op jit(solution)/shard_map/all_to_all | solution.py:56
  318.3 7.1 %reshape.234 = bf16[640,1,961]{2,1,0:T(2,128)(2,1)} reshape(bf16[16,2,19220]{2,1,0:T(2,128)(2,1)} %all_to_all.21) | data formatting | bytes 2460160
  325.4 3.5 copy.17
  328.8 8.5 %bitcast_reduce_fusion = bf16[640,961]{1,0:T(8,128)(2,1)} fusion(bf16[640,1,961]{2,1,0:T(2,128)(2,1)S(1)} %copy-done.1), kind=kLoop, calls=%fused_computation.32 | loop fusion | bytes 2460160 | tf_op jit(solution)/shard_map/all_to_all | solution.py:56
  337.3 3.9 reshape.227
  341.2 39.0 %reshape.231 = bf16[256,38440]{1,0:T(8,128)(2,1)} reshape(bf16[256,40,961]{2,1,0:T(8,128)(2,1)} %all-gather.2.cloned.1.call-done) | data formatting | bytes 39362560 | tf_op jit(solution)/shard_map/reshape | solution.py:63
  380.2 10.5 %convolution_multiply_fusion = f32[256,16]{1,0:T(8,128)} fusion(bf16[256,38440]{1,0:T(8,128)(2,1)} %reshape.231, bf16[16,38440]{1,0:T(8,128)(2,1)} %reshape.227), kind=kOutput, calls=%fused_computation.28 | convolution fusion | flops 314904576 | bytes 20927744 | tf_op jit(solution)/shard_map/dot_general | solution.py:62
  390.7 0.0 reduce-scatter.2.cloned.1.call-update
  390.7 4.4 convolution_convert_fusion
  395.1 63.7 %reduce-scatter.2.cloned.1.call-done = f32[16,16]{1,0:T(8,128)} async-done(((f32[256,16]{1,0:T(8,128)}), f32[16,16]{1,0:T(8,128)}) %reduce-scatter.2.cloned.1.call-update) | async-done | bytes 1040 | tf_op jit(solution)/shard_map/reduce_scatter | solution.py:70
  (7 shorter events, 0.0 us)
Async XLA Ops:
  7.2 1.7 copy-start
  7.2 334.1 %all-gather.2.cloned.1.call-start = ((), (), s32[]{:S(2)}) async-start(), calls=%async_computation.3 | async-start | bytes 22282240 | tf_op jit(solution)/shard_map/all_gather | solution.py:61
  13.3 31.8 %all-to-all-start = ((bf16[16,40,961]{2,1,0:T(8,128)(2,1)}), bf16[16,40,961]{2,1,0:T(8,128)(2,1)}, u32[]{:S(2)}, u32[]{:S(2)}) async-start(bf16[16,40,961]{2,1,0:T(8,128)(2,1)} %multiply_convert_fusion.1), calls=%async_computation | async-start | bytes 2621440 | tf_op jit(solution)/shard_map/all_to_all | solution.py:48
  21.7 437.1 %reduce-scatter.2.cloned.1.call-start = ((), (), s32[]{:S(2)}) async-start(), calls=%async_computation.4 | async-start | bytes 139264 | tf_op jit(solution)/shard_map/reduce_scatter | solution.py:70
  48.4 1.7 copy-start.3
  50.1 6.6 %copy-start.2 = (f32[1,640,961]{1,2,0:T(8,128)S(1)}, f32[1,640,961]{1,2,0:T(8,128)}, u32[]{:S(2)}) copy-start(f32[1,640,961]{1,2,0:T(8,128)} %copy.13) | copy-start | bytes 7380484
  50.1 6.6 %copy-start.4 = (f32[961]{0:T(1024)S(1)}, f32[961]{0:T(1024)}, u32[]{:S(2)}) copy-start(f32[961]{0:T(1024)} %constant.33) | copy-start | bytes 11536
  50.1 6.6 %copy-start.5 = (f32[961]{0:T(1024)S(1)}, f32[961]{0:T(1024)}, u32[]{:S(2)}) copy-start(f32[961]{0:T(1024)} %constant.32) | copy-start | bytes 11536
  325.4 3.5 copy-start.1
Sparse Core Ops, SparseCore 0:
  13.4 236.6 all-gather.1
  390.8 67.9 reduce-scatter.1
where the time goes:
time: 471 us; the launch traced here: 466 us
  blocking collectives  230 us (49%)
  waiting for transfers between devices  87 us (18%)
  local copies, waits for them, and re-layouts  78.4 us (17%)
  matrix products  34.4 us (7%)
  between operations  14.4 us (3%)
  other arithmetic  13.5 us (3%)
  starting transfers between devices  8.53 us (2%)
    all_to_all x1, blocking collectives, local(): lax.all_to_all(grouped, 'rad', split_axis=1, concat_axis=0, tiled=True)  230 us
    reduce_scatter x1, waiting for transfers between devices, local(): lax.psum_scatter(partial_kernel, 'rad', scatter_dimension=0, tiled=True)  63.7 us
    reshape x1, local copies, waits for them, and re-layouts, local(): piece.reshape(piece.shape[0], -1)  39 us
    all_to_all x1, waiting for transfers between devices, local(): lax.all_to_all(weighted, 'rad', split_axis=0, concat_axis=1, tiled=True)  23.3 us
    unnamed x16, local copies, waits for them, and re-layouts  17.4 us
    unnamed x1, other arithmetic  11 us
    dot_general x1, matrix products, local(): lax.dot_general(piece.reshape(piece.shape[0], -1), flat_coefficients, (((...  10.5 us
  transfers between devices with their start and end apart: 3, of which 2 were waited for; matrix products, arithmetic and copies ran while one was open for 15% of the time, Pallas kernels for 0%

commit v1 on v0

v1 whole, which is shorter than its diff:
```python
import functools
import math

import jax
import jax.numpy as jnp
from jax import lax
from jax.experimental import pallas as pl
from jax.experimental.pallas import tpu as pltpu
from jax.sharding import PartitionSpec as P

MESH = pl.DeviceIdType.MESH
F32, BF16 = jnp.float32, jnp.bfloat16
ANGLES, HARM, RADII = 1202, 961, 640
RADS, FNS = 16, 16
ROWS, FUNCS = 40, 16
SPACING = 3.0 / RADII
CHUNKS, WIDE = 4, 256
TILES = 2 * ROWS // FNS
FN_STEPS = [(y, z) for z in (4, 3, 5, 2, 6, 1, 7, 0) for y in (0, 1) if (y, z) != (0, 0)]


def degree_of(first, width):
    m = first + lax.broadcasted_iota(jnp.int32, (1, width), 1)
    return jnp.floor(jnp.sqrt(m.astype(F32) + 0.5))


def kernel(
    functions, orbital, weight, ylm,
    potential, matrix,
    fn_v, orb_v, ylm_v, dens, proj, src, inw, coef, pot_v,
    decay, rise, scale, fall, couple_o, couple_n,
    y_buf, y_in, x_buf, x_in, edge, edge_in, gram, part_in, slab, slab_in,
    load_sem, store_sem, y_send, y_recv, x_send, x_recv, e_send, e_recv, p_send, p_recv, s_send, s_recv,
):
    rad, fn = lax.axis_index("rad"), lax.axis_index("fn")
    fn_y, fn_z = fn // 8, lax.rem(fn, 8)
    fn_peers = [lax.rem(fn_y + y, 2) * 8 + lax.rem(fn_z + z, 8) for y, z in FN_STEPS]

    loads = [
        pltpu.make_async_copy(functions, fn_v, load_sem.at[0]),
        pltpu.make_async_copy(orbital, orb_v, load_sem.at[1]),
        pltpu.make_async_copy(ylm, ylm_v, load_sem.at[2]),
    ]
    for copy in loads:
        copy.start()

    barrier = pltpu.get_barrier_semaphore()
    for peer in fn_peers:
        pl.semaphore_signal(barrier, inc=1, device_id=(rad, peer), device_id_type=MESH)

    @pl.loop(1, RADS)
    def _(step):
        pl.semaphore_signal(barrier, inc=1, device_id=(lax.rem(rad + step, RADS), fn), device_id_type=MESH)

    def radius_of(position):
        return 1.0 + SPACING * (position.astype(F32) + 0.5)

    def minus_log(x):
        return x * (1.0 + x * (0.5 + x * (1.0 / 3.0 + x * 0.25)))

    rows = lax.broadcasted_iota(jnp.int32, (ROWS, 1), 0)
    radius = radius_of(rad * ROWS + rows)
    gap = SPACING / radius
    step_log = minus_log(gap)
    next_log = minus_log(SPACING / radius_of(rad * ROWS + rows + 1))
    for c in range(CHUNKS):
        lanes = pl.ds(c * WIDE, WIDE)
        deg = degree_of(c * WIDE, WIDE)
        decay[:, lanes] = jnp.exp(-deg * next_log)
        rise[:, lanes] = jnp.exp(-deg * step_log) * (1.0 - gap)
        t = (2.0 * deg + 1.0) * step_log
        em = t * (1.0 - t * (1 / 2) * (1.0 - t * (1 / 3) * (1.0 - t * (1 / 4) * (1.0 - t * (1 / 5) * (1.0 - t * (1 / 6) * (1.0 - t * (1 / 7)))))))
        em = jnp.where(rows == 0, 1.0, em)
        scale[:, lanes] = jnp.sqrt((16.0 * math.pi**2 / ANGLES) / (2.0 * deg + 1.0) * radius * em)

    for copy in loads[:2]:
        copy.wait()
    orb = orb_v[...]

    @pl.loop(0, FUNCS // 2)
    def _(pair):
        d = fn_v[pl.ds(2 * pair, 2)].astype(F32) * orb[None]
        dens[pl.ds(pl.multiple_of(pair * 80, 16), 80), :] = d.reshape(80, ANGLES).astype(BF16)

    loads[2].wait()

    for c in range(CHUNKS):
        width = min(WIDE, HARM - c * WIDE)
        out = lax.dot_general(
            dens[...], ylm_v[c * WIDE:c * WIDE + width, :], (((1,), (1,)), ((), ())), preferred_element_type=F32
        )
        if width == WIDE:
            proj[0] = out[:, :128]
            proj[1] = out[:, 128:]
        else:
            proj[0] = out[:, :128]
            proj[1] = jnp.zeros_like(proj[1])
            proj[1, :, 0:width - 128] = out[:, 128:]

        base = c * WIDE

        def back(step, n):
            first_row = pl.multiple_of(8 * (ROWS // 8 - 1 - step), 8)
            down = decay[pl.ds(first_row, 8), base:base + WIDE]
            up = scale[pl.ds(first_row, 8), base:base + WIDE]
            for k in reversed(range(8)):
                i = first_row + k
                r_i = 1.0 + SPACING * ((rad * ROWS + i).astype(F32) + 0.5)
                factor = SPACING * weight[i] * r_i
                new = []
                for h in range(2):
                    lanes = slice(128 * h, 128 * h + 128)
                    s = proj[h, pl.ds(i, FUNCS, stride=ROWS), :] * factor
                    src[2 * c + h, i] = s
                    v = s + down[k:k + 1, lanes] * n[h]
                    inw[2 * c + h, i] = v
                    y_buf[c, 2 * i + h] = (v * up[k:k + 1, lanes]).astype(BF16)
                    new.append(v)
                n = tuple(new)
            return n

        zero = jnp.zeros((FUNCS, 128), F32)
        first = lax.fori_loop(0, ROWS // 8, back, (zero, zero))
        for h in range(2):
            edge[1, :, base + 128 * h:base + 128 * h + 128] = first[h].astype(BF16)

        if c == 0:
            pl.semaphore_wait(barrier, len(FN_STEPS) + RADS - 1)
        for peer in fn_peers:
            pltpu.make_async_remote_copy(
                src_ref=y_buf.at[c, pl.ds(peer * TILES, TILES)],
                dst_ref=y_in.at[c, fn],
                send_sem=y_send.at[c, peer],
                recv_sem=y_recv.at[c, fn],
                device_id=(rad, peer),
                device_id_type=MESH,
            ).start()
        y_in[c, fn] = y_buf[c, pl.ds(fn * TILES, TILES)]

        def forth(step, o):
            first_row = pl.multiple_of(8 * step, 8)
            up = rise[pl.ds(first_row, 8), base:base + WIDE]
            for k in range(8):
                o = tuple(
                    src[2 * c + h, first_row + k] + up[k:k + 1, 128 * h:128 * h + 128] * o[h] for h in range(2)
                )
            return o

        last = lax.fori_loop(0, ROWS // 8, forth, (zero, zero))
        for h in range(2):
            edge[0, :, base + 128 * h:base + 128 * h + 128] = last[h].astype(BF16)

    @pl.loop(1, RADS)
    def _(step):
        peer = lax.rem(rad + step, RADS)
        pltpu.make_async_remote_copy(
            src_ref=edge.at[jnp.where(peer > rad, 0, 1)],
            dst_ref=edge_in.at[rad],
            send_sem=e_send.at[peer],
            recv_sem=e_recv.at[rad],
            device_id=(peer, fn),
            device_id_type=MESH,
        ).start()

    edge_in[rad] = jnp.zeros((FUNCS, CHUNKS * WIDE), BF16)
    blocks = lax.broadcasted_iota(jnp.int32, (RADS, 1), 0)
    log_last = jnp.log(radius_of(blocks * ROWS + (ROWS - 1)))
    log_first = jnp.log(radius_of(blocks * ROWS))
    spot = jnp.full((1, 1), rad, jnp.int32)
    log_end = jnp.log(radius_of(spot * ROWS - 1))
    log_next = jnp.log(radius_of(spot * ROWS + ROWS))
    log_row = jnp.log(radius)
    for c in range(CHUNKS):
        lanes = pl.ds(c * WIDE, WIDE)
        deg = degree_of(c * WIDE, WIDE)
        couple_o[:, lanes] = jnp.where(blocks < spot, jnp.exp((deg + 1.0) * jnp.minimum(log_last - log_end, 0.0)), 0.0)
        couple_n[:, lanes] = jnp.where(blocks > spot, jnp.exp(deg * jnp.minimum(log_next - log_first, 0.0)), 0.0)
        fall[:, lanes] = jnp.exp(deg * jnp.minimum(log_row - log_next, 0.0))

    @pl.loop(1, RADS)
    def _(step):
        peer = lax.rem(rad + step, RADS)
        pltpu.make_async_remote_copy(
            src_ref=edge.at[0], dst_ref=edge_in.at[peer], send_sem=e_send.at[peer], recv_sem=e_recv.at[peer],
            device_id=(peer, fn), device_id_type=MESH,
        ).wait_recv()

    lane = lax.broadcasted_iota(jnp.int32, (FUNCS, 128), 1)
    for t in range(2 * CHUNKS):
        lanes = slice(128 * t, 128 * t + 128)
        out_carry = jnp.zeros((FUNCS, 128), F32)
        in_carry = jnp.zeros((FUNCS, 128), F32)
        for b in range(RADS):
            e = edge_in[b, :, lanes].astype(F32)
            out_carry = out_carry + couple_o[b:b + 1, lanes] * e
            in_carry = in_carry + couple_n[b:b + 1, lanes] * e
        a_tile = inw[t, 0] * scale[0:1, lanes]
        p_tile = out_carry * (scale[0:1, lanes] * rise[0:1, lanes])
        x_buf[2 * t] = jnp.where(lane < 64, a_tile, pltpu.roll(p_tile, 64, 1)).astype(BF16)
        x_buf[2 * t + 1] = jnp.where(lane < 64, pltpu.roll(a_tile, 64, 1), p_tile).astype(BF16)
        multipole = (4.0 * math.pi) / (2.0 * degree_of(128 * t, 128) + 1.0)

        def forth(step, o):
            first_row = pl.multiple_of(8 * step, 8)
            up = rise[pl.ds(first_row, 8), lanes]
            far = fall[pl.ds(first_row, 8), lanes]
            for k in range(8):
                i = first_row + k
                grown = up[k:k + 1] * o
                total = grown + inw[t, i] + far[k:k + 1] * in_carry
                coef[t, pl.ds(i, FUNCS, stride=ROWS), :] = multipole * total
                o = grown + src[t, i]
            return o

        lax.fori_loop(0, ROWS // 8, forth, out_carry)

    for peer in fn_peers:
        pltpu.make_async_remote_copy(
            src_ref=x_buf.at[peer], dst_ref=x_in.at[fn], send_sem=x_send.at[peer], recv_sem=x_recv.at[fn],
            device_id=(rad, peer), device_id_type=MESH,
        ).start()
    x_in[fn] = x_buf[fn]

    @pl.loop(0, FUNCS // 4)
    def _(quad):
        at = pl.ds(pl.multiple_of(quad * 160, 16), 160)
        left = jnp.concatenate([coef[t, at, :].astype(BF16) for t in range(2 * CHUNKS)], axis=1)[:, :HARM]
        out = jnp.dot(left, ylm_v[...], preferred_element_type=F32)
        pot_v[pl.ds(4 * quad, 4)] = out.reshape(4, ROWS, ANGLES).astype(BF16)

    store = pltpu.make_async_copy(pot_v, potential, store_sem)
    store.start()

    def gram_of(left, right):
        return lax.dot_general(left, right, (((1,), (1,)), ((), ())), preferred_element_type=F32)

    for c in range(CHUNKS):
        for peer in fn_peers:
            pltpu.make_async_remote_copy(
                src_ref=y_buf.at[c, pl.ds(0, TILES)], dst_ref=y_in.at[c, peer], send_sem=y_send.at[c, peer],
                recv_sem=y_recv.at[c, peer], device_id=(rad, peer), device_id_type=MESH,
            ).wait_recv()
        x = jnp.concatenate([y_in[c, :, t].reshape(FNS * FUNCS, 128) for t in range(TILES)], axis=1)
        if c == 0:
            gram[...] = gram_of(x, x)
        else:
            gram[...] += gram_of(x, x)

    for peer in fn_peers:
        pltpu.make_async_remote_copy(
            src_ref=x_buf.at[peer], dst_ref=x_in.at[peer], send_sem=x_send.at[peer], recv_sem=x_recv.at[peer],
            device_id=(rad, peer), device_id_type=MESH,
        ).wait_recv()
    x = x_in[...].reshape(FNS * FUNCS, 128)
    gram[...] += gram_of(x, jnp.concatenate([x[:, 64:], x[:, :64]], axis=1))

    def part_copy(peer, slot):
        return pltpu.make_async_remote_copy(
            src_ref=gram.at[pl.ds(pl.multiple_of(peer * FUNCS, 8), FUNCS)], dst_ref=part_in.at[slot],
            send_sem=p_send.at[peer], recv_sem=p_recv.at[slot], device_id=(peer, fn), device_id_type=MESH,
        )

    @pl.loop(1, RADS)
    def _(step):
        part_copy(lax.rem(rad + step, RADS), rad).start()

    part_in[rad] = gram[pl.ds(pl.multiple_of(rad * FUNCS, 8), FUNCS), :]

    @pl.loop(1, RADS)
    def _(step):
        peer = lax.rem(rad + step, RADS)
        part_copy(peer, peer).wait_recv()

    total = part_in[0]
    for b in range(1, RADS):
        total = total + part_in[b]
    slab[0] = total[:, :128]
    slab[1] = total[:, 128:]

    def slab_copy(peer, slot):
        return pltpu.make_async_remote_copy(
            src_ref=slab.at[peer // 8], dst_ref=slab_in.at[slot], send_sem=s_send.at[peer],
            recv_sem=s_recv.at[slot], device_id=(rad, peer), device_id_type=MESH,
        )

    for peer in fn_peers:
        slab_copy(peer, fn).start()
    slab_in[fn] = slab[fn // 8]
    for peer in fn_peers:
        slab_copy(peer, peer).wait_recv()
    total = slab_in[0]
    for b in range(1, FNS):
        total = total + slab_in[b]
    shift = lax.rem(128 - 16 * lax.rem(fn, 8), 128)
    matrix[...] = pltpu.roll(total, shift, 1)[:, :FUNCS]

    for peer in fn_peers:
        for c in range(CHUNKS):
            pltpu.make_async_remote_copy(
                src_ref=y_buf.at[c, pl.ds(peer * TILES, TILES)], dst_ref=y_in.at[c, fn], send_sem=y_send.at[c, peer],
                recv_sem=y_recv.at[c, fn], device_id=(rad, peer), device_id_type=MESH,
            ).wait_send()
        pltpu.make_async_remote_copy(
            src_ref=x_buf.at[peer], dst_ref=x_in.at[fn], send_sem=x_send.at[peer], recv_sem=x_recv.at[fn],
            device_id=(rad, peer), device_id_type=MESH,
        ).wait_send()
        slab_copy(peer, fn).wait_send()

    @pl.loop(1, RADS)
    def _(step):
        peer = lax.rem(rad + step, RADS)
        pltpu.make_async_remote_copy(
            src_ref=edge.at[0], dst_ref=edge_in.at[rad], send_sem=e_send.at[peer], recv_sem=e_recv.at[rad],
            device_id=(peer, fn), device_id_type=MESH,
        ).wait_send()
        part_copy(peer, rad).wait_send()

    store.wait()


def local(functions, orbital, radial_weight, ylm):
    any_ = pl.BlockSpec(memory_space=pl.ANY)
    vmem, dma = pltpu.VMEM, pltpu.SemaphoreType.DMA
    lanes = CHUNKS * WIDE
    return pl.pallas_call(
        kernel,
        out_shape=(
            jax.ShapeDtypeStruct((FUNCS, ROWS, ANGLES), BF16),
            jax.ShapeDtypeStruct((FUNCS, FUNCS), F32),
        ),
        in_specs=[any_, any_, pl.BlockSpec(memory_space=pltpu.SMEM), any_],
        out_specs=(any_, pl.BlockSpec(memory_space=pltpu.VMEM)),
        scratch_shapes=[
            vmem((FUNCS, ROWS, ANGLES), BF16),
            vmem((ROWS, ANGLES), F32),
            vmem((HARM, ANGLES), BF16),
            vmem((FUNCS * ROWS, ANGLES), BF16),
            vmem((2, FUNCS * ROWS, 128), F32),
            vmem((2 * CHUNKS, ROWS, FUNCS, 128), F32),
            vmem((2 * CHUNKS, ROWS, FUNCS, 128), F32),
            vmem((2 * CHUNKS, FUNCS * ROWS, 128), F32),
            vmem((FUNCS, ROWS, ANGLES), BF16),
            vmem((ROWS, lanes), F32),
            vmem((ROWS, lanes), F32),
            vmem((ROWS, lanes), F32),
            vmem((ROWS, lanes), F32),
            vmem((RADS, lanes), F32),
            vmem((RADS, lanes), F32),
            vmem((CHUNKS, 2 * ROWS, FUNCS, 128), BF16),
            vmem((CHUNKS, FNS, TILES, FUNCS, 128), BF16),
            vmem((FNS, FUNCS, 128), BF16),
            vmem((FNS, FUNCS, 128), BF16),
            vmem((2, FUNCS, lanes), BF16),
            vmem((RADS, FUNCS, lanes), BF16),
            vmem((FNS * FUNCS, FNS * FUNCS), F32),
            vmem((RADS, FUNCS, FNS * FUNCS), F32),
            vmem((2, FUNCS, 128), F32),
            vmem((FNS, FUNCS, 128), F32),
            dma((3,)), dma(()),
            dma((CHUNKS, FNS)), dma((CHUNKS, FNS)),
            dma((FNS,)), dma((FNS,)),
            dma((RADS,)), dma((RADS,)),
            dma((RADS,)), dma((RADS,)),
            dma((FNS,)), dma((FNS,)),
        ],
        compiler_params=pltpu.CompilerParams(
            collective_id=0, has_side_effects=True, vmem_limit_bytes=48 * 2**20
        ),
    )(functions, orbital, radial_weight, ylm)


def solution(mesh):
    in_specs = (P("fn", "rad", None), P("rad", None), P("rad"), P())
    out_specs = (P("fn", "rad", None), P("rad", "fn"))
    return jax.shard_map(local, mesh=mesh, in_specs=in_specs, out_specs=out_specs, check_vma=False)
```

time: 471 us -> 66.1 us (0.14); the launches traced: 466 us -> 65.9 us
  blocking collectives: 230 us -> 0 us
  waiting for transfers between devices: 87 us -> 0 us
  local copies, waits for them, and re-layouts: 78.4 us -> 6.44 us
  Pallas kernels: 0 us -> 58.8 us
  matrix products: 34.4 us -> 0 us
  between operations: 14.4 us -> 0.69 us
  other arithmetic: 13.5 us -> 0 us
  starting transfers between devices: 8.53 us -> 0 us
    all_to_all x1 -> x0, blocking collectives: 230 us -> none  [local(): lax.all_to_all(grouped, 'rad', split_axis=1, concat_axis=0, tiled=True)]
    reduce_scatter x1 -> x0, waiting for transfers between devices: 63.7 us -> none  [local(): lax.psum_scatter(partial_kernel, 'rad', scatter_dimension=0, tiled=True)]
    pallas_call x0 -> x1, Pallas kernels: none -> 58.8 us  [local(): pl.pallas_call(kernel, out_shape=(jax.ShapeDtypeStruct((FUNCS, ROWS, ANGL...]
    reshape x2 -> x0, local copies, waits for them, and re-layouts: 42.9 us -> none  [the longest x1 39 us: local(): piece.reshape(piece.shape[0], -1)]
    dot_general x5 -> x0, matrix products: 34.4 us -> none  [the longest x1 10.5 us: local(): lax.dot_general(piece.reshape(piece.shape[0], -1), flat_coefficients, (((...]
    all_to_all x1 -> x0, waiting for transfers between devices: 23.3 us -> none  [local(): lax.all_to_all(weighted, 'rad', split_axis=0, concat_axis=1, tiled=True)]
    unnamed x1 -> x0, other arithmetic: 11 us -> none
    unnamed x16 -> x9, local copies, waits for them, and re-layouts: 17.4 us -> 6.44 us
  transfers between devices with their start and end apart: 3 -> 0, of which waited for: 2 -> 0; matrix products, arithmetic and copies ran while one was open for 15% -> 0% of each run, Pallas kernels for 0% -> 0%
where the time goes in v1:
time: 66.1 us; the launch traced here: 65.9 us
  Pallas kernels  58.8 us (89%)
  local copies, waits for them, and re-layouts  6.44 us (10%)
  between operations  0.69 us (1%)
    pallas_call x1, Pallas kernels, local(): pl.pallas_call(kernel, out_shape=(jax.ShapeDtypeStruct((FUNCS, ROWS, ANGL...  58.8 us
    unnamed x9, local copies, waits for them, and re-layouts  6.44 us

profile of v1, /device:TPU:1, one launch (start us, length us, event | category | flops | bytes accessed | tf_op | source)
XLA Modules:
  0.0 65.9 jit_solution(14305704881630801116)
XLA Ops:
  0.6 0.0 copy-start.2
  0.6 0.0 copy-start.1
  0.7 3.2 %copy.6.ylm = bf16[961,1202]{1,0:T(8,128)(2,1)S(1)} copy(bf16[961,1202]{0,1:T(8,128)(2,1)} %param.7) | data formatting | bytes 4620488 | tf_op args[3]
  3.9 0.0 copy-done.2
  3.9 0.0 copy-done.1
  3.9 0.0 copy-start
  3.9 1.4 %copy-done = bf16[16,40,1202]{2,1,0:T(8,128)(2,1)S(1)} copy-done((bf16[16,40,1202]{2,1,0:T(8,128)(2,1)S(1)}, bf16[16,40,1202]{2,1,0:T(8,128)(2,1)}, u32[]{:S(2)}) %copy-start) | copy-done | bytes 1538584
  5.4 58.8 %shard_map.59 = (bf16[16,40,1202]{2,1,0:T(8,128)(2,1)S(1)}, f32[16,16]{1,0:T(8,128)S(1)}) custom-call(bf16[16,40,1202]{2,1,0:T(8,128)(2,1)S(1)} %copy-done, f32[40,1202]{1,0:T(8,128)S(1)} %copy-done.1, f32[40]{0:T(128)S(1)} %copy-done.2, bf16[961,1202]{1,0:T(8,128)(2,1)S(1)} %copy.6.ylm), custom_call_target="tpu_custom_call" | custom-call | tf_op jit(solution)/shard_map/pallas_call | solution.py:325
  64.2 1.2 %copy.9 = bf16[16,40,1202]{2,1,0:T(8,128)(2,1)} copy(bf16[16,40,1202]{2,1,0:T(8,128)(2,1)S(1)} %get-tuple-element.4) | data formatting | bytes 3077120
  65.3 0.6 copy.10
Async XLA Ops:
  0.6 3.3 %copy-start.2 = (f32[40]{0:T(128)S(1)}, f32[40]{0:T(128)}, u32[]{:S(2)}) copy-start(f32[40]{0:T(128)} %weight.1) | copy-start | bytes 484
  0.6 3.3 %copy-start.1 = (f32[40,1202]{1,0:T(8,128)S(1)}, f32[40,1202]{1,0:T(8,128)}, u32[]{:S(2)}) copy-start(f32[40,1202]{1,0:T(8,128)} %orbital.1) | copy-start | bytes 576964
  3.9 1.4 %copy-start = (bf16[16,40,1202]{2,1,0:T(8,128)(2,1)S(1)}, bf16[16,40,1202]{2,1,0:T(8,128)(2,1)}, u32[]{:S(2)}) copy-start(bf16[16,40,1202]{2,1,0:T(8,128)(2,1)} %functions.1) | copy-start | bytes 4615684

commit v2 on v1

--- a/solution.py
+++ b/solution.py
@@ -15,7 +15,7 @@
 ROWS, FUNCS = 40, 16
 SPACING = 3.0 / RADII
 CHUNKS, WIDE = 4, 256
-TILES = 2 * ROWS // FNS
+TILES = (5, 5, 5, 4)
 FN_STEPS = [(y, z) for z in (4, 3, 5, 2, 6, 1, 7, 0) for y in (0, 1) if (y, z) != (0, 0)]
 
 
@@ -24,13 +24,24 @@
     return jnp.floor(jnp.sqrt(m.astype(F32) + 0.5))
 
 
+def swap_blocks(x):
+    row = lax.broadcasted_iota(jnp.int32, (8, 128), 0)
+    block = lax.broadcasted_iota(jnp.int32, (8, 128), 1) // 16
+    for b in (1, 2, 4):
+        row_bit, block_bit = (row // b) % 2, (block // b) % 2
+        above = pltpu.roll(pltpu.roll(x, 8 - b, 0), 16 * b, 1)
+        below = pltpu.roll(pltpu.roll(x, b, 0), 128 - 16 * b, 1)
+        x = jnp.where(row_bit == block_bit, x, jnp.where(block_bit == 1, above, below))
+    return x
+
+
 def kernel(
     functions, orbital, weight, ylm,
     potential, matrix,
-    fn_v, orb_v, ylm_v, dens, proj, src, inw, coef, pot_v,
+    fn_v, orb_v, ylm_v, dens, proj, src, inw, coef,
     decay, rise, scale, fall, couple_o, couple_n,
-    y_buf, y_in, x_buf, x_in, edge, edge_in, gram, part_in, slab, slab_in,
-    load_sem, store_sem, y_send, y_recv, x_send, x_recv, e_send, e_recv, p_send, p_recv, s_send, s_recv,
+    y_buf, y_in, x_buf, x_in, edge, edge_in, gram, part, part_in, slab, slab_in,
+    load_sem, y_send, y_recv, x_send, x_recv, e_send, e_recv, p_send, p_recv, s_send, s_recv,
 ):
     rad, fn = lax.axis_index("rad"), lax.axis_index("fn")
     fn_y, fn_z = fn // 8, lax.rem(fn, 8)
@@ -51,6 +62,12 @@
     @pl.loop(1, RADS)
     def _(step):
         pl.semaphore_signal(barrier, inc=1, device_id=(lax.rem(rad + step, RADS), fn), device_id_type=MESH)
+
+    def y_copy(c, peer, slot):
+        return pltpu.make_async_remote_copy(
+            src_ref=y_buf.at[c, pl.ds(peer * TILES[c], TILES[c])], dst_ref=y_in.at[c, slot, pl.ds(0, TILES[c])],
+            send_sem=y_send.at[c, peer], recv_sem=y_recv.at[c, slot], device_id=(rad, peer), device_id_type=MESH,
+        )
 
     def radius_of(position):
         return 1.0 + SPACING * (position.astype(F32) + 0.5)
@@ -84,10 +101,11 @@
 
     loads[2].wait()
 
+    lane = lax.broadcasted_iota(jnp.int32, (FUNCS, 128), 1)
     for c in range(CHUNKS):
         width = min(WIDE, HARM - c * WIDE)
         out = lax.dot_general(
-            dens[...], ylm_v[c * WIDE:c * WIDE + width, :], (((1,), (1,)), ((), ())), preferred_element_type=F32
+            dens[...], ylm_v[:, c * WIDE:c * WIDE + width], (((1,), (0,)), ((), ())), preferred_element_type=F32
         )
         if width == WIDE:
             proj[0] = out[:, :128]
@@ -99,7 +117,8 @@
 
         base = c * WIDE
 
-        def back(step, n):
+        def back(step, carry):
+            n, spare = carry
             first_row = pl.multiple_of(8 * (ROWS // 8 - 1 - step), 8)
             down = decay[pl.ds(first_row, 8), base:base + WIDE]
             up = scale[pl.ds(first_row, 8), base:base + WIDE]
@@ -114,28 +133,34 @@
                     src[2 * c + h, i] = s
                     v = s + down[k:k + 1, lanes] * n[h]
                     inw[2 * c + h, i] = v
-                    y_buf[c, 2 * i + h] = (v * up[k:k + 1, lanes]).astype(BF16)
+                    y = v * up[k:k + 1, lanes]
+                    if width == WIDE:
+                        y_buf[c, 2 * i + h] = y.astype(BF16)
+                    elif h == 0:
+                        y_buf[c, i] = y.astype(BF16)
+                    else:
+                        spare = jnp.where(lane == i, y[:, 64:65], spare)
+                        if k % 2:
+                            odd = pltpu.roll(y, 64, 1)
+                        else:
+                            y_buf[c, ROWS + first_row // 2 + k // 2] = jnp.where(lane < 64, y, odd).astype(BF16)
                     new.append(v)
                 n = tuple(new)
-            return n
+            return n, spare
 
         zero = jnp.zeros((FUNCS, 128), F32)
-        first = lax.fori_loop(0, ROWS // 8, back, (zero, zero))
+        first, spare = lax.fori_loop(0, ROWS // 8, back, ((zero, zero), zero))
+        if width < WIDE:
+            y_buf[c, ROWS + ROWS // 2] = spare.astype(BF16)
+            y_buf[c, ROWS + ROWS // 2 + 1:FNS * TILES[c]] = jnp.zeros((3, FUNCS, 128), BF16)
         for h in range(2):
             edge[1, :, base + 128 * h:base + 128 * h + 128] = first[h].astype(BF16)
 
         if c == 0:
             pl.semaphore_wait(barrier, len(FN_STEPS) + RADS - 1)
         for peer in fn_peers:
-            pltpu.make_async_remote_copy(
-                src_ref=y_buf.at[c, pl.ds(peer * TILES, TILES)],
-                dst_ref=y_in.at[c, fn],
-                send_sem=y_send.at[c, peer],
-                recv_sem=y_recv.at[c, fn],
-                device_id=(rad, peer),
-                device_id_type=MESH,
-            ).start()
-        y_in[c, fn] = y_buf[c, pl.ds(fn * TILES, TILES)]
+            y_copy(c, peer, fn).start()
+        y_in[c, fn, 0:TILES[c]] = y_buf[c, pl.ds(fn * TILES[c], TILES[c])]
 
         def forth(step, o):
             first_row = pl.multiple_of(8 * step, 8)
@@ -185,7 +210,6 @@
             device_id=(peer, fn), device_id_type=MESH,
         ).wait_recv()
 
-    lane = lax.broadcasted_iota(jnp.int32, (FUNCS, 128), 1)
     for t in range(2 * CHUNKS):
         lanes = slice(128 * t, 128 * t + 128)
         out_carry = jnp.zeros((FUNCS, 128), F32)
@@ -225,22 +249,16 @@
     def _(quad):
         at = pl.ds(pl.multiple_of(quad * 160, 16), 160)
         left = jnp.concatenate([coef[t, at, :].astype(BF16) for t in range(2 * CHUNKS)], axis=1)[:, :HARM]
-        out = jnp.dot(left, ylm_v[...], preferred_element_type=F32)
-        pot_v[pl.ds(4 * quad, 4)] = out.reshape(4, ROWS, ANGLES).astype(BF16)
-
-    store = pltpu.make_async_copy(pot_v, potential, store_sem)
-    store.start()
+        out = lax.dot_general(left, ylm_v[...], (((1,), (1,)), ((), ())), preferred_element_type=F32)
+        potential[pl.ds(4 * quad, 4)] = out.reshape(4, ROWS, ANGLES).astype(BF16)
 
     def gram_of(left, right):
         return lax.dot_general(left, right, (((1,), (1,)), ((), ())), preferred_element_type=F32)
 
     for c in range(CHUNKS):
         for peer in fn_peers:
-            pltpu.make_async_remote_copy(
-                src_ref=y_buf.at[c, pl.ds(0, TILES)], dst_ref=y_in.at[c, peer], send_sem=y_send.at[c, peer],
-                recv_sem=y_recv.at[c, peer], device_id=(rad, peer), device_id_type=MESH,
-            ).wait_recv()
-        x = jnp.concatenate([y_in[c, :, t].reshape(FNS * FUNCS, 128) for t in range(TILES)], axis=1)
+            y_copy(c, peer, peer).wait_recv()
+        x = jnp.concatenate([y_in[c, :, t].reshape(FNS * FUNCS, 128) for t in range(TILES[c])], axis=1)
         if c == 0:
             gram[...] = gram_of(x, x)
         else:
@@ -252,11 +270,11 @@
             device_id=(rad, peer), device_id_type=MESH,
         ).wait_recv()
     x = x_in[...].reshape(FNS * FUNCS, 128)
-    gram[...] += gram_of(x, jnp.concatenate([x[:, 64:], x[:, :64]], axis=1))
+    part[...] = (gram[...] + gram_of(x, jnp.concatenate([x[:, 64:], x[:, :64]], axis=1))).astype(BF16)
 
     def part_copy(peer, slot):
         return pltpu.make_async_remote_copy(
-            src_ref=gram.at[pl.ds(pl.multiple_of(peer * FUNCS, 8), FUNCS)], dst_ref=part_in.at[slot],
+            src_ref=part.at[pl.ds(pl.multiple_of(peer * FUNCS, 16), FUNCS)], dst_ref=part_in.at[slot],
             send_sem=p_send.at[peer], recv_sem=p_recv.at[slot], device_id=(peer, fn), device_id_type=MESH,
         )
 
@@ -264,42 +282,43 @@
     def _(step):
         part_copy(lax.rem(rad + step, RADS), rad).start()
 
-    part_in[rad] = gram[pl.ds(pl.multiple_of(rad * FUNCS, 8), FUNCS), :]
+    part_in[rad] = part[pl.ds(pl.multiple_of(rad * FUNCS, 16), FUNCS), :]
 
     @pl.loop(1, RADS)
     def _(step):
         peer = lax.rem(rad + step, RADS)
         part_copy(peer, peer).wait_recv()
 
-    total = part_in[0]
+    total = part_in[0].astype(F32)
     for b in range(1, RADS):
-        total = total + part_in[b]
-    slab[0] = total[:, :128]
-    slab[1] = total[:, 128:]
+        total = total + part_in[b].astype(F32)
+    for h in range(2):
+        for q in range(2):
+            tile = swap_blocks(total[8 * h:8 * h + 8, 128 * q:128 * q + 128])
+            for k in range(8):
+                slab[8 * q + k, h:h + 1, :] = tile[k:k + 1, :]
 
     def slab_copy(peer, slot):
         return pltpu.make_async_remote_copy(
-            src_ref=slab.at[peer // 8], dst_ref=slab_in.at[slot], send_sem=s_send.at[peer],
+            src_ref=slab.at[peer], dst_ref=slab_in.at[slot], send_sem=s_send.at[peer],
             recv_sem=s_recv.at[slot], device_id=(rad, peer), device_id_type=MESH,
         )
 
     for peer in fn_peers:
         slab_copy(peer, fn).start()
-    slab_in[fn] = slab[fn // 8]
+    slab_in[fn] = slab[fn]
     for peer in fn_peers:
         slab_copy(peer, peer).wait_recv()
     total = slab_in[0]
     for b in range(1, FNS):
         total = total + slab_in[b]
-    shift = lax.rem(128 - 16 * lax.rem(fn, 8), 128)
-    matrix[...] = pltpu.roll(total, shift, 1)[:, :FUNCS]
+    for h in range(2):
+        tile = swap_blocks(jnp.broadcast_to(total[h:h + 1], (8, 128)))
+        matrix[8 * h:8 * h + 8, :] = tile[:, :FUNCS]
 
     for peer in fn_peers:
         for c in range(CHUNKS):
-            pltpu.make_async_remote_copy(
-                src_ref=y_buf.at[c, pl.ds(peer * TILES, TILES)], dst_ref=y_in.at[c, fn], send_sem=y_send.at[c, peer],
-                recv_sem=y_recv.at[c, fn], device_id=(rad, peer), device_id_type=MESH,
-            ).wait_send()
+            y_copy(c, peer, fn).wait_send()
         pltpu.make_async_remote_copy(
             src_ref=x_buf.at[peer], dst_ref=x_in.at[fn], send_sem=x_send.at[peer], recv_sem=x_recv.at[fn],
             device_id=(rad, peer), device_id_type=MESH,
@@ -315,31 +334,25 @@
         ).wait_send()
         part_copy(peer, rad).wait_send()
 
-    store.wait()
-
 
 def local(functions, orbital, radial_weight, ylm):
-    any_ = pl.BlockSpec(memory_space=pl.ANY)
+    hbm = pl.BlockSpec(memory_space=pltpu.HBM)
     vmem, dma = pltpu.VMEM, pltpu.SemaphoreType.DMA
     lanes = CHUNKS * WIDE
     return pl.pallas_call(
         kernel,
-        out_shape=(
-            jax.ShapeDtypeStruct((FUNCS, ROWS, ANGLES), BF16),
-            jax.ShapeDtypeStruct((FUNCS, FUNCS), F32),
-        ),
-        in_specs=[any_, any_, pl.BlockSpec(memory_space=pltpu.SMEM), any_],
-        out_specs=(any_, pl.BlockSpec(memory_space=pltpu.VMEM)),
+        out_shape=(vmem((FUNCS, ROWS, ANGLES), BF16), vmem((FUNCS, FUNCS), F32)),
+        in_specs=[hbm, hbm, pl.BlockSpec(memory_space=pltpu.SMEM), hbm],
+        out_specs=(pl.BlockSpec(memory_space=pltpu.VMEM), pl.BlockSpec(memory_space=pltpu.VMEM)),
         scratch_shapes=[
             vmem((FUNCS, ROWS, ANGLES), BF16),
             vmem((ROWS, ANGLES), F32),
-            vmem((HARM, ANGLES), BF16),
+            vmem((ANGLES, HARM), BF16),
             vmem((FUNCS * ROWS, ANGLES), BF16),
             vmem((2, FUNCS * ROWS, 128), F32),
             vmem((2 * CHUNKS, ROWS, FUNCS, 128), F32),
             vmem((2 * CHUNKS, ROWS, FUNCS, 128), F32),
             vmem((2 * CHUNKS, FUNCS * ROWS, 128), F32),
-            vmem((FUNCS, ROWS, ANGLES), BF16),
             vmem((ROWS, lanes), F32),
             vmem((ROWS, lanes), F32),
             vmem((ROWS, lanes), F32),
@@ -347,16 +360,17 @@
             vmem((RADS, lanes), F32),
             vmem((RADS, lanes), F32),
             vmem((CHUNKS, 2 * ROWS, FUNCS, 128), BF16),
-            vmem((CHUNKS, FNS, TILES, FUNCS, 128), BF16),
+            vmem((CHUNKS, FNS, max(TILES), FUNCS, 128), BF16),
             vmem((FNS, FUNCS, 128), BF16),
             vmem((FNS, FUNCS, 128), BF16),
             vmem((2, FUNCS, lanes), BF16),
             vmem((RADS, FUNCS, lanes), BF16),
             vmem((FNS * FUNCS, FNS * FUNCS), F32),
-            vmem((RADS, FUNCS, FNS * FUNCS), F32),
-            vmem((2, FUNCS, 128), F32),
-            vmem((FNS, FUNCS, 128), F32),
-            dma((3,)), dma(()),
+            vmem((FNS * FUNCS, FNS * FUNCS), BF16),
+            vmem((RADS, FUNCS, FNS * FUNCS), BF16),
+            vmem((FNS, 2, 128), F32),
+            vmem((FNS, 2, 128), F32),
+            dma((3,)),
             dma((CHUNKS, FNS)), dma((CHUNKS, FNS)),
             dma((FNS,)), dma((FNS,)),
             dma((RADS,)), dma((RADS,)),
@@ -364,9 +378,9 @@
             dma((FNS,)), dma((FNS,)),
         ],
         compiler_params=pltpu.CompilerParams(
-            collective_id=0, has_side_effects=True, vmem_limit_bytes=48 * 2**20
+            collective_id=0, has_side_effects=True, vmem_limit_bytes=61 * 2**20
         ),
-    )(functions, orbital, radial_weight, ylm)
+    )(functions, orbital, radial_weight, ylm.T)
 
 
 def solution(mesh):

time: 66.1 us -> 58.2 us (0.88)
  local copies, waits for them, and re-layouts: 6.44 us -> 1.76 us
  Pallas kernels: 58.8 us -> 55.7 us
    unnamed x9 -> x2, local copies, waits for them, and re-layouts: 6.44 us -> 1.76 us
    pallas_call x1, Pallas kernels: 58.8 us -> 55.7 us  [local(): pl.pallas_call(kernel, out_shape=(vmem((FUNCS, ROWS, ANGLES), BF16), vmem...]
where the time goes in v2:
time: 58.2 us; the launch traced here: 58.1 us
  Pallas kernels  55.7 us (96%)
  local copies, waits for them, and re-layouts  1.76 us (3%)
  between operations  0.64 us (1%)
    pallas_call x1, Pallas kernels, local(): pl.pallas_call(kernel, out_shape=(vmem((FUNCS, ROWS, ANGLES), BF16), vmem...  55.7 us
    unnamed x2, local copies, waits for them, and re-layouts  1.76 us

profile of v2, /device:TPU:1, one launch (start us, length us, event | category | flops | bytes accessed | tf_op | source)
XLA Modules:
  0.0 58.1 jit_solution(16965395077845835634)
XLA Ops:
  0.6 55.7 %shard_map.59 = (bf16[16,40,1202]{2,1,0:T(8,128)(2,1)S(1)}, f32[16,16]{1,0:T(8,128)S(1)}) custom-call(bf16[16,40,1202]{2,1,0:T(8,128)(2,1)} %functions.1, f32[40,1202]{1,0:T(8,128)} %orbital.1, f32[40]{0:T(128)} %weight.1, bf16[1202,961]{1,0:T(8,128)(2,1)} %bitcast.1), custom_call_target="tpu_custom_call" | custom-call | tf_op jit(solution)/shard_map/pallas_call | solution.py:342
  56.3 1.2 %copy.8 = bf16[16,40,1202]{2,1,0:T(8,128)(2,1)} copy(bf16[16,40,1202]{2,1,0:T(8,128)(2,1)S(1)} %get-tuple-element.2) | data formatting | bytes 3077120
  57.5 0.6 %copy.9 = f32[16,16]{1,0:T(8,128)} copy(f32[16,16]{1,0:T(8,128)S(1)} %get-tuple-element.3) | data formatting | bytes 2048

commit v3 on v2

--- a/solution.py
+++ b/solution.py
@@ -16,12 +16,16 @@
 SPACING = 3.0 / RADII
 CHUNKS, WIDE = 4, 256
 TILES = (5, 5, 5, 4)
+OWN = 3
 FN_STEPS = [(y, z) for z in (4, 3, 5, 2, 6, 1, 7, 0) for y in (0, 1) if (y, z) != (0, 0)]
 
 
 def degree_of(first, width):
     m = first + lax.broadcasted_iota(jnp.int32, (1, width), 1)
     return jnp.floor(jnp.sqrt(m.astype(F32) + 0.5))
+
+
+RAD_STEPS = (8, 7, 9, 6, 10, 5, 11, 4, 12, 3, 13, 2, 14, 1, 15)
 
 
 def swap_blocks(x):
@@ -52,9 +56,6 @@
         pltpu.make_async_copy(orbital, orb_v, load_sem.at[1]),
         pltpu.make_async_copy(ylm, ylm_v, load_sem.at[2]),
     ]
-    for copy in loads:
-        copy.start()
-
     barrier = pltpu.get_barrier_semaphore()
     for peer in fn_peers:
         pl.semaphore_signal(barrier, inc=1, device_id=(rad, peer), device_id_type=MESH)
@@ -63,10 +64,28 @@
     def _(step):
         pl.semaphore_signal(barrier, inc=1, device_id=(lax.rem(rad + step, RADS), fn), device_id_type=MESH)
 
+    for copy in loads:
+        copy.start()
+
+    core = lax.rem(rad, 2)
+
+    def share(c, peer):
+        y, z = peer // 8, lax.rem(peer, 8)
+        return y * 8 + lax.rem(z + 4 * y + 6 * core + 8 - c, 8)
+
+    def first_owner(c, h):
+        return h * 8 + lax.rem(4 * h + 2 * core + c, 8)
+
     def y_copy(c, peer, slot):
         return pltpu.make_async_remote_copy(
-            src_ref=y_buf.at[c, pl.ds(peer * TILES[c], TILES[c])], dst_ref=y_in.at[c, slot, pl.ds(0, TILES[c])],
+            src_ref=y_buf.at[c, pl.ds(share(c, peer) * TILES[c], TILES[c])], dst_ref=y_in.at[c, slot, pl.ds(0, TILES[c])],
             send_sem=y_send.at[c, peer], recv_sem=y_recv.at[c, slot], device_id=(rad, peer), device_id_type=MESH,
+        )
+
+    def x_copy(t, peer, slot):
+        return pltpu.make_async_remote_copy(
+            src_ref=x_buf.at[t], dst_ref=x_in.at[slot], send_sem=x_send.at[t], recv_sem=x_recv.at[slot],
+            device_id=(rad, peer), device_id_type=MESH,
         )
 
     def radius_of(position):
@@ -87,7 +106,7 @@
         rise[:, lanes] = jnp.exp(-deg * step_log) * (1.0 - gap)
         t = (2.0 * deg + 1.0) * step_log
         em = t * (1.0 - t * (1 / 2) * (1.0 - t * (1 / 3) * (1.0 - t * (1 / 4) * (1.0 - t * (1 / 5) * (1.0 - t * (1 / 6) * (1.0 - t * (1 / 7)))))))
-        em = jnp.where(rows == 0, 1.0, em)
+        em = jnp.where(rows + (0 if c < OWN else rad * ROWS) == 0, 1.0, em)
         scale[:, lanes] = jnp.sqrt((16.0 * math.pi**2 / ANGLES) / (2.0 * deg + 1.0) * radius * em)
 
     for copy in loads[:2]:
@@ -102,6 +121,24 @@
     loads[2].wait()
 
     lane = lax.broadcasted_iota(jnp.int32, (FUNCS, 128), 1)
+
+    def put_tiles(c, first_row, k, ys, odd, spare):
+        i = first_row + k
+        if c < CHUNKS - 1:
+            for h in range(2):
+                y_buf[c, ROWS * h + i] = ys[h].astype(BF16)
+            return odd, spare
+        y_buf[c, i] = ys[0].astype(BF16)
+        spare = jnp.where(lane == i, ys[1][:, 64:65], spare)
+        if k % 2:
+            y_buf[c, ROWS + first_row // 2 + k // 2] = jnp.where(lane < 64, odd, pltpu.roll(ys[1], 64, 1)).astype(BF16)
+        return ys[1], spare
+
+    def send_chunk(c):
+        for peer in fn_peers:
+            y_copy(c, peer, fn).start()
+        y_in[c, fn, 0:TILES[c]] = y_buf[c, pl.ds(share(c, fn) * TILES[c], TILES[c])]
+
     for c in range(CHUNKS):
         width = min(WIDE, HARM - c * WIDE)
         out = lax.dot_general(
@@ -117,8 +154,7 @@
 
         base = c * WIDE
 
-        def back(step, carry):
-            n, spare = carry
+        def back(step, n):
             first_row = pl.multiple_of(8 * (ROWS // 8 - 1 - step), 8)
             down = decay[pl.ds(first_row, 8), base:base + WIDE]
             up = scale[pl.ds(first_row, 8), base:base + WIDE]
@@ -133,34 +169,21 @@
                     src[2 * c + h, i] = s
                     v = s + down[k:k + 1, lanes] * n[h]
                     inw[2 * c + h, i] = v
-                    y = v * up[k:k + 1, lanes]
-                    if width == WIDE:
-                        y_buf[c, 2 * i + h] = y.astype(BF16)
-                    elif h == 0:
-                        y_buf[c, i] = y.astype(BF16)
-                    else:
-                        spare = jnp.where(lane == i, y[:, 64:65], spare)
-                        if k % 2:
-                            odd = pltpu.roll(y, 64, 1)
-                        else:
-                            y_buf[c, ROWS + first_row // 2 + k // 2] = jnp.where(lane < 64, y, odd).astype(BF16)
                     new.append(v)
+                if c < OWN:
+                    put_tiles(c, first_row, k, [new[h] * up[k:k + 1, 128 * h:128 * h + 128] for h in range(2)], None, None)
                 n = tuple(new)
-            return n, spare
+            return n
 
         zero = jnp.zeros((FUNCS, 128), F32)
-        first, spare = lax.fori_loop(0, ROWS // 8, back, ((zero, zero), zero))
-        if width < WIDE:
-            y_buf[c, ROWS + ROWS // 2] = spare.astype(BF16)
-            y_buf[c, ROWS + ROWS // 2 + 1:FNS * TILES[c]] = jnp.zeros((3, FUNCS, 128), BF16)
+        first = lax.fori_loop(0, ROWS // 8, back, (zero, zero))
         for h in range(2):
             edge[1, :, base + 128 * h:base + 128 * h + 128] = first[h].astype(BF16)
 
         if c == 0:
             pl.semaphore_wait(barrier, len(FN_STEPS) + RADS - 1)
-        for peer in fn_peers:
-            y_copy(c, peer, fn).start()
-        y_in[c, fn, 0:TILES[c]] = y_buf[c, pl.ds(fn * TILES[c], TILES[c])]
+        if c < OWN:
+            send_chunk(c)
 
         def forth(step, o):
             first_row = pl.multiple_of(8 * step, 8)
@@ -210,6 +233,7 @@
             device_id=(peer, fn), device_id_type=MESH,
         ).wait_recv()
 
+    carries = []
     for t in range(2 * CHUNKS):
         lanes = slice(128 * t, 128 * t + 128)
         out_carry = jnp.zeros((FUNCS, 128), F32)
@@ -218,11 +242,48 @@
             e = edge_in[b, :, lanes].astype(F32)
             out_carry = out_carry + couple_o[b:b + 1, lanes] * e
             in_carry = in_carry + couple_n[b:b + 1, lanes] * e
-        a_tile = inw[t, 0] * scale[0:1, lanes]
-        p_tile = out_carry * (scale[0:1, lanes] * rise[0:1, lanes])
-        x_buf[2 * t] = jnp.where(lane < 64, a_tile, pltpu.roll(p_tile, 64, 1)).astype(BF16)
-        x_buf[2 * t + 1] = jnp.where(lane < 64, pltpu.roll(a_tile, 64, 1), p_tile).astype(BF16)
+        carries.append((out_carry, in_carry))
+        if t < 2 * OWN:
+            x_buf[t] = (out_carry * (scale[0:1, lanes] * rise[0:1, lanes])).astype(BF16)
+
+    for c in range(OWN, CHUNKS):
+        base = c * WIDE
+
+        def whole(step, spare):
+            first_row = pl.multiple_of(8 * step, 8)
+            up = scale[pl.ds(first_row, 8), base:base + WIDE]
+            far = fall[pl.ds(first_row, 8), base:base + WIDE]
+            odd = None
+            for k in range(8):
+                ys = []
+                for h in range(2):
+                    lanes = slice(128 * h, 128 * h + 128)
+                    v = inw[2 * c + h, first_row + k] + far[k:k + 1, lanes] * carries[2 * c + h][1]
+                    ys.append(v * up[k:k + 1, lanes])
+                odd, spare = put_tiles(c, first_row, k, ys, odd, spare)
+            return spare
+
+        spare = lax.fori_loop(0, ROWS // 8, whole, jnp.zeros((FUNCS, 128), F32))
+        if c == CHUNKS - 1:
+            y_buf[c, ROWS + ROWS // 2] = spare.astype(BF16)
+            y_buf[c, ROWS + ROWS // 2 + 1:FNS * TILES[c]] = jnp.zeros((3, FUNCS, 128), BF16)
+        send_chunk(c)
+        if c == OWN:
+            for t in range(2 * OWN):
+                owner = first_owner(t // 2, t % 2)
+
+                @pl.when(owner != fn)
+                def _():
+                    x_copy(t, owner, fn).start()
+
+                @pl.when(owner == fn)
+                def _():
+                    x_in[fn] = x_buf[t]
+
+    for t in range(2 * CHUNKS):
+        lanes = slice(128 * t, 128 * t + 128)
         multipole = (4.0 * math.pi) / (2.0 * degree_of(128 * t, 128) + 1.0)
+        out_carry, in_carry = carries[t]
 
         def forth(step, o):
             first_row = pl.multiple_of(8 * step, 8)
@@ -238,13 +299,6 @@
 
         lax.fori_loop(0, ROWS // 8, forth, out_carry)
 
-    for peer in fn_peers:
-        pltpu.make_async_remote_copy(
-            src_ref=x_buf.at[peer], dst_ref=x_in.at[fn], send_sem=x_send.at[peer], recv_sem=x_recv.at[fn],
-            device_id=(rad, peer), device_id_type=MESH,
-        ).start()
-    x_in[fn] = x_buf[fn]
-
     @pl.loop(0, FUNCS // 4)
     def _(quad):
         at = pl.ds(pl.multiple_of(quad * 160, 16), 160)
@@ -261,16 +315,20 @@
         x = jnp.concatenate([y_in[c, :, t].reshape(FNS * FUNCS, 128) for t in range(TILES[c])], axis=1)
         if c == 0:
             gram[...] = gram_of(x, x)
+        elif c < CHUNKS - 1:
+            gram[...] += gram_of(x, x)
         else:
-            gram[...] += gram_of(x, x)
-
-    for peer in fn_peers:
-        pltpu.make_async_remote_copy(
-            src_ref=x_buf.at[peer], dst_ref=x_in.at[peer], send_sem=x_send.at[peer], recv_sem=x_recv.at[peer],
-            device_id=(rad, peer), device_id_type=MESH,
-        ).wait_recv()
-    x = x_in[...].reshape(FNS * FUNCS, 128)
-    part[...] = (gram[...] + gram_of(x, jnp.concatenate([x[:, 64:], x[:, :64]], axis=1))).astype(BF16)
+            part[...] = (gram[...] + gram_of(x, x)).astype(BF16)
+        if c == CHUNKS - 2:
+            for t in range(2 * OWN):
+
+                @pl.when(first_owner(t // 2, t % 2) == fn)
+                def _():
+                    for peer in fn_peers:
+                        x_copy(t, peer, peer).wait_recv()
+                    p = x_in[...].reshape(FNS * FUNCS, 128)
+                    a = y_in[t // 2, :, 0].reshape(FNS * FUNCS, 128)
+                    gram[...] += gram_of(a, p) + gram_of(p, a)
 
     def part_copy(peer, slot):
         return pltpu.make_async_remote_copy(
@@ -278,15 +336,13 @@
             send_sem=p_send.at[peer], recv_sem=p_recv.at[slot], device_id=(peer, fn), device_id_type=MESH,
         )
 
-    @pl.loop(1, RADS)
-    def _(step):
-        part_copy(lax.rem(rad + step, RADS), rad).start()
+    rad_peers = [lax.rem(rad + step, RADS) for step in RAD_STEPS]
+    for peer in rad_peers:
+        part_copy(peer, rad).start()
 
     part_in[rad] = part[pl.ds(pl.multiple_of(rad * FUNCS, 16), FUNCS), :]
 
-    @pl.loop(1, RADS)
-    def _(step):
-        peer = lax.rem(rad + step, RADS)
+    for peer in rad_peers:
         part_copy(peer, peer).wait_recv()
 
     total = part_in[0].astype(F32)
@@ -319,11 +375,13 @@
     for peer in fn_peers:
         for c in range(CHUNKS):
             y_copy(c, peer, fn).wait_send()
-        pltpu.make_async_remote_copy(
-            src_ref=x_buf.at[peer], dst_ref=x_in.at[fn], send_sem=x_send.at[peer], recv_sem=x_recv.at[fn],
-            device_id=(rad, peer), device_id_type=MESH,
-        ).wait_send()
         slab_copy(peer, fn).wait_send()
+    for t in range(2 * OWN):
+        owner = first_owner(t // 2, t % 2)
+
+        @pl.when(owner != fn)
+        def _():
+            x_copy(t, owner, fn).wait_send()
 
     @pl.loop(1, RADS)
     def _(step):
@@ -361,7 +419,7 @@
             vmem((RADS, lanes), F32),
             vmem((CHUNKS, 2 * ROWS, FUNCS, 128), BF16),
             vmem((CHUNKS, FNS, max(TILES), FUNCS, 128), BF16),
-            vmem((FNS, FUNCS, 128), BF16),
+            vmem((2 * OWN, FUNCS, 128), BF16),
             vmem((FNS, FUNCS, 128), BF16),
             vmem((2, FUNCS, lanes), BF16),
             vmem((RADS, FUNCS, lanes), BF16),
@@ -372,7 +430,7 @@
             vmem((FNS, 2, 128), F32),
             dma((3,)),
             dma((CHUNKS, FNS)), dma((CHUNKS, FNS)),
-            dma((FNS,)), dma((FNS,)),
+            dma((2 * OWN,)), dma((FNS,)),
             dma((RADS,)), dma((RADS,)),
             dma((RADS,)), dma((RADS,)),
             dma((FNS,)), dma((FNS,)),

time: 58.2 us -> 57.3 us (0.985)
  Pallas kernels: 55.7 us -> 54.8 us
    pallas_call x1, Pallas kernels: 55.7 us -> 54.8 us  [local(): pl.pallas_call(kernel, out_shape=(vmem((FUNCS, ROWS, ANGLES), BF16), vmem...]
where the time goes in v3:
time: 57.3 us; the launch traced here: 57.2 us
  Pallas kernels  54.8 us (96%)
  local copies, waits for them, and re-layouts  1.76 us (3%)
  between operations  0.64 us (1%)
    pallas_call x1, Pallas kernels, local(): pl.pallas_call(kernel, out_shape=(vmem((FUNCS, ROWS, ANGLES), BF16), vmem...  54.8 us
    unnamed x2, local copies, waits for them, and re-layouts  1.76 us

profile of v3, /device:TPU:1, one launch (start us, length us, event | category | flops | bytes accessed | tf_op | source)
XLA Modules:
  0.0 57.2 jit_solution(10743763063366199266)
XLA Ops:
  0.6 54.8 %shard_map.59 = (bf16[16,40,1202]{2,1,0:T(8,128)(2,1)S(1)}, f32[16,16]{1,0:T(8,128)S(1)}) custom-call(bf16[16,40,1202]{2,1,0:T(8,128)(2,1)} %functions.1, f32[40,1202]{1,0:T(8,128)} %orbital.1, f32[40]{0:T(128)} %weight.1, bf16[1202,961]{1,0:T(8,128)(2,1)} %bitcast.1), custom_call_target="tpu_custom_call" | custom-call | tf_op jit(solution)/shard_map/pallas_call | solution.py:400
  55.4 1.2 %copy.8 = bf16[16,40,1202]{2,1,0:T(8,128)(2,1)} copy(bf16[16,40,1202]{2,1,0:T(8,128)(2,1)S(1)} %get-tuple-element.2) | data formatting | bytes 3077120
  56.6 0.6 %copy.9 = f32[16,16]{1,0:T(8,128)} copy(f32[16,16]{1,0:T(8,128)S(1)} %get-tuple-element.3) | data formatting | bytes 2048

commit v4 on v3

--- a/solution.py
+++ b/solution.py
@@ -306,6 +306,14 @@
         out = lax.dot_general(left, ylm_v[...], (((1,), (1,)), ((), ())), preferred_element_type=F32)
         potential[pl.ds(4 * quad, 4)] = out.reshape(4, ROWS, ANGLES).astype(BF16)
 
+    @pl.loop(1, RADS)
+    def _(step):
+        peer = lax.rem(rad + step, RADS)
+        pltpu.make_async_remote_copy(
+            src_ref=edge.at[0], dst_ref=edge_in.at[rad], send_sem=e_send.at[peer], recv_sem=e_recv.at[rad],
+            device_id=(peer, fn), device_id_type=MESH,
+        ).wait_send()
+
     def gram_of(left, right):
         return lax.dot_general(left, right, (((1,), (1,)), ((), ())), preferred_element_type=F32)
 
@@ -340,6 +348,17 @@
     for peer in rad_peers:
         part_copy(peer, rad).start()
 
+    for c in range(CHUNKS):
+        for peer in fn_peers:
+            y_copy(c, peer, fn).wait_send()
+    for t in range(2 * OWN):
+        owner = first_owner(t // 2, t % 2)
+
+        @pl.when(owner != fn)
+        def _():
+            x_copy(t, owner, fn).wait_send()
+
+
     part_in[rad] = part[pl.ds(pl.multiple_of(rad * FUNCS, 16), FUNCS), :]
 
     for peer in rad_peers:
@@ -362,6 +381,8 @@
 
     for peer in fn_peers:
         slab_copy(peer, fn).start()
+    for peer in rad_peers:
+        part_copy(peer, rad).wait_send()
     slab_in[fn] = slab[fn]
     for peer in fn_peers:
         slab_copy(peer, peer).wait_recv()
@@ -373,24 +394,7 @@
         matrix[8 * h:8 * h + 8, :] = tile[:, :FUNCS]
 
     for peer in fn_peers:
-        for c in range(CHUNKS):
-            y_copy(c, peer, fn).wait_send()
         slab_copy(peer, fn).wait_send()
-    for t in range(2 * OWN):
-        owner = first_owner(t // 2, t % 2)
-
-        @pl.when(owner != fn)
-        def _():
-            x_copy(t, owner, fn).wait_send()
-
-    @pl.loop(1, RADS)
-    def _(step):
-        peer = lax.rem(rad + step, RADS)
-        pltpu.make_async_remote_copy(
-            src_ref=edge.at[0], dst_ref=edge_in.at[rad], send_sem=e_send.at[peer], recv_sem=e_recv.at[rad],
-            device_id=(peer, fn), device_id_type=MESH,
-        ).wait_send()
-        part_copy(peer, rad).wait_send()
 
 
 def local(functions, orbital, radial_weight, ylm):

time: 57.3 us -> 57 us (level)
  no operation moved by 1% of the time
where the time goes in v4:
time: 57 us; the launch traced here: 56.9 us
  Pallas kernels  54.5 us (96%)
  local copies, waits for them, and re-layouts  1.76 us (3%)
  between operations  0.64 us (1%)
    pallas_call x1, Pallas kernels, local(): pl.pallas_call(kernel, out_shape=(vmem((FUNCS, ROWS, ANGLES), BF16), vmem...  54.5 us
    unnamed x2, local copies, waits for them, and re-layouts  1.76 us

profile of v4, /device:TPU:1, one launch (start us, length us, event | category | flops | bytes accessed | tf_op | source)
XLA Modules:
  0.0 56.9 jit_solution(2160375286863735308)
XLA Ops:
  0.6 54.5 %shard_map.59 = (bf16[16,40,1202]{2,1,0:T(8,128)(2,1)S(1)}, f32[16,16]{1,0:T(8,128)S(1)}) custom-call(bf16[16,40,1202]{2,1,0:T(8,128)(2,1)} %functions.1, f32[40,1202]{1,0:T(8,128)} %orbital.1, f32[40]{0:T(128)} %weight.1, bf16[1202,961]{1,0:T(8,128)(2,1)} %bitcast.1), custom_call_target="tpu_custom_call" | custom-call | tf_op jit(solution)/shard_map/pallas_call | solution.py:404
  55.1 1.2 %copy.8 = bf16[16,40,1202]{2,1,0:T(8,128)(2,1)} copy(bf16[16,40,1202]{2,1,0:T(8,128)(2,1)S(1)} %get-tuple-element.2) | data formatting | bytes 3077120
  56.3 0.6 %copy.9 = f32[16,16]{1,0:T(8,128)} copy(f32[16,16]{1,0:T(8,128)S(1)} %get-tuple-element.3) | data formatting | bytes 2048

commit v5 on v4

--- a/solution.py
+++ b/solution.py
@@ -359,14 +359,12 @@
             x_copy(t, owner, fn).wait_send()
 
 
-    part_in[rad] = part[pl.ds(pl.multiple_of(rad * FUNCS, 16), FUNCS), :]
+    total = part[pl.ds(pl.multiple_of(rad * FUNCS, 16), FUNCS), :].astype(F32)
 
     for peer in rad_peers:
         part_copy(peer, peer).wait_recv()
-
-    total = part_in[0].astype(F32)
-    for b in range(1, RADS):
-        total = total + part_in[b].astype(F32)
+        total = total + part_in[peer].astype(F32)
+
     for h in range(2):
         for q in range(2):
             tile = swap_blocks(total[8 * h:8 * h + 8, 128 * q:128 * q + 128])
@@ -383,12 +381,10 @@
         slab_copy(peer, fn).start()
     for peer in rad_peers:
         part_copy(peer, rad).wait_send()
-    slab_in[fn] = slab[fn]
+    total = slab[fn]
     for peer in fn_peers:
         slab_copy(peer, peer).wait_recv()
-    total = slab_in[0]
-    for b in range(1, FNS):
-        total = total + slab_in[b]
+        total = total + slab_in[peer]
     for h in range(2):
         tile = swap_blocks(jnp.broadcast_to(total[h:h + 1], (8, 128)))
         matrix[8 * h:8 * h + 8, :] = tile[:, :FUNCS]

time: 57 us -> 57 us (level)
  no operation moved by 1% of the time
where the time goes in v5:
time: 57 us; the launch traced here: 56.9 us
  Pallas kernels  54.5 us (96%)
  local copies, waits for them, and re-layouts  1.76 us (3%)
  between operations  0.64 us (1%)
    pallas_call x1, Pallas kernels, local(): pl.pallas_call(kernel, out_shape=(vmem((FUNCS, ROWS, ANGLES), BF16), vmem...  54.5 us
    unnamed x2, local copies, waits for them, and re-layouts  1.76 us

profile of v5, /device:TPU:1, one launch (start us, length us, event | category | flops | bytes accessed | tf_op | source)
XLA Modules:
  0.0 56.9 jit_solution(3157967000116165528)
XLA Ops:
  0.6 54.5 %shard_map.59 = (bf16[16,40,1202]{2,1,0:T(8,128)(2,1)S(1)}, f32[16,16]{1,0:T(8,128)S(1)}) custom-call(bf16[16,40,1202]{2,1,0:T(8,128)(2,1)} %functions.1, f32[40,1202]{1,0:T(8,128)} %orbital.1, f32[40]{0:T(128)} %weight.1, bf16[1202,961]{1,0:T(8,128)(2,1)} %bitcast.1), custom_call_target="tpu_custom_call" | custom-call | tf_op jit(solution)/shard_map/pallas_call | solution.py:400
  55.1 1.2 %copy.8 = bf16[16,40,1202]{2,1,0:T(8,128)(2,1)} copy(bf16[16,40,1202]{2,1,0:T(8,128)(2,1)S(1)} %get-tuple-element.2) | data formatting | bytes 3077120
  56.3 0.6 %copy.9 = f32[16,16]{1,0:T(8,128)} copy(f32[16,16]{1,0:T(8,128)S(1)} %get-tuple-element.3) | data formatting | bytes 2048

commit v6 on v5

--- a/solution.py
+++ b/solution.py
@@ -318,6 +318,9 @@
         return lax.dot_general(left, right, (((1,), (1,)), ((), ())), preferred_element_type=F32)
 
     for c in range(CHUNKS):
+        if c > 0:
+            for peer in fn_peers:
+                y_copy(c - 1, peer, fn).wait_send()
         for peer in fn_peers:
             y_copy(c, peer, peer).wait_recv()
         x = jnp.concatenate([y_in[c, :, t].reshape(FNS * FUNCS, 128) for t in range(TILES[c])], axis=1)
@@ -348,9 +351,8 @@
     for peer in rad_peers:
         part_copy(peer, rad).start()
 
-    for c in range(CHUNKS):
-        for peer in fn_peers:
-            y_copy(c, peer, fn).wait_send()
+    for peer in fn_peers:
+        y_copy(CHUNKS - 1, peer, fn).wait_send()
     for t in range(2 * OWN):
         owner = first_owner(t // 2, t % 2)
 

time: 57 us -> 57 us (level)
  no operation moved by 1% of the time
where the time goes in v6:
time: 57 us; the launch traced here: 56.9 us
  Pallas kernels  54.5 us (96%)
  local copies, waits for them, and re-layouts  1.76 us (3%)
  between operations  0.64 us (1%)
    pallas_call x1, Pallas kernels, local(): pl.pallas_call(kernel, out_shape=(vmem((FUNCS, ROWS, ANGLES), BF16), vmem...  54.5 us
    unnamed x2, local copies, waits for them, and re-layouts  1.76 us

profile of v6, /device:TPU:1, one launch (start us, length us, event | category | flops | bytes accessed | tf_op | source)
XLA Modules:
  0.0 56.9 jit_solution(3590179555153192237)
XLA Ops:
  0.6 54.5 %shard_map.59 = (bf16[16,40,1202]{2,1,0:T(8,128)(2,1)S(1)}, f32[16,16]{1,0:T(8,128)S(1)}) custom-call(bf16[16,40,1202]{2,1,0:T(8,128)(2,1)} %functions.1, f32[40,1202]{1,0:T(8,128)} %orbital.1, f32[40]{0:T(128)} %weight.1, bf16[1202,961]{1,0:T(8,128)(2,1)} %bitcast.1), custom_call_target="tpu_custom_call" | custom-call | tf_op jit(solution)/shard_map/pallas_call | solution.py:402
  55.1 1.2 %copy.8 = bf16[16,40,1202]{2,1,0:T(8,128)(2,1)} copy(bf16[16,40,1202]{2,1,0:T(8,128)(2,1)S(1)} %get-tuple-element.2) | data formatting | bytes 3077120
  56.3 0.6 %copy.9 = f32[16,16]{1,0:T(8,128)} copy(f32[16,16]{1,0:T(8,128)S(1)} %get-tuple-element.3) | data formatting | bytes 2048
